TPU v7x, 32 devices: a whole 2x2x4 slice. The times are simulated.
32 devices in a mesh: groups: 2 (over y), loop: 4 (over z), band: 2 (over x), win: 2 (over core).
Axes of the slice: x: 2, y: 2, z: 4, core: 2. Of those that a mesh axis runs over, the one named last changes fastest.
Arguments:
- spectra_phase: bfloat16 [8, 512, 1280], P(('groups', 'win'), 'band', 'loop'), parts along dimension 0, may hold values from -3.140625 to 3.140625
- window_valid: int32 [8, 1280], P('groups', 'loop'), parts along dimension 0, may hold values 0 or 1
- band_gain: float32 [512], P('band'), may hold values from 0.02 to 0.2
- cross_index: int32 [2560, 8], P(('groups', 'loop')), parts along dimension 0, may hold values from 0 to 319
Outputs:
- coherence: float32 [2560, 2, 320], P(('groups', 'loop', 'band', 'win')), parts along dimension 0
- crossing: float32 [2560, 8], P(('groups', 'loop', 'band', 'win')), parts along dimension 0
There are 2 independent parts, one for each index of `groups`. A program takes and returns all parts, laid end to end along the dimension named above; an argument that names none is the same for every part. Nothing has to cross between parts.
Inputs may be any that keep to these rules, and one draw needn't show every extreme that they name: `window_valid`: 1 marks a usable window of a channel, 0 a rejected one. `cross_index`: each entry is a channel position within the opposite block.
All inputs are finite; a program needn't handle non-finite values. No bound on the sum of `window_valid` on one device may be relied on, other than what follows from the above.
Results may differ from a plain program's by a relative error of at most 0.0037.
Values may be sent and summed in bfloat16 or wider, within the bound.
A program may use at most 64 MiB of HBM per device.

v0:
```python
import jax
import jax.numpy as jnp
from jax import lax
from jax.sharding import PartitionSpec as P


def passed_along(value, axis, steps):
    count = lax.axis_size(axis)
    pairs = [(source, (source + steps) % count) for source in range(count)]
    return lax.ppermute(value, axis, pairs)


def swapped(value, axis, distance):
    mask = 2**distance
    pairs = [(source, source ^ mask) for source in range(lax.axis_size(axis))]
    return lax.ppermute(value, axis, pairs)


def unpack(packet, win_dev, freq_dev, win_slot):
    phase_rows = win_dev * freq_dev
    phases = packet[:phase_rows].reshape(win_dev, freq_dev, packet.shape[1])
    all_flags = packet[phase_rows:]
    valid_rows = lax.dynamic_slice_in_dim(all_flags, win_slot * win_dev, win_dev, 0)
    return (phases, valid_rows, all_flags)


def trig_rows(phases, factor):
    values = phases.astype(jnp.float32)
    stacked = jnp.stack([jnp.cos(values) * factor, jnp.sin(values) * factor])
    return stacked.astype(jnp.bfloat16).reshape(-1, phases.shape[-1])


def on_device(spectra_phase, window_valid, band_gain, cross_index):
    win_dev, freq_dev, channels_dev = spectra_phase.shape
    far_reach = lax.axis_size("loop") // 4
    offset_count = far_reach + 1
    win_slot = lax.axis_index("win")
    valid_flags = window_valid.astype(jnp.bfloat16)
    packet = jnp.concatenate(
        [spectra_phase.reshape(win_dev * freq_dev, channels_dev), valid_flags], axis=0
    )
    packets = [packet]
    current = packet
    for offset in range(far_reach):
        current = passed_along(current, "loop", -1)
        packets.append(current)
    opposite = swapped(packet, "loop", lax.axis_size("loop").bit_length() - 2)
    far_sides = []
    far_flag_rows = []
    for held in packets + [opposite]:
        phases, valid_rows, all_flags = unpack(held, win_dev, freq_dev, win_slot)
        far_sides.append(trig_rows(phases, valid_rows.astype(jnp.float32)[:, None, :]))
        far_flag_rows.append(all_flags)
    far_joined = jnp.concatenate(far_sides, axis=1)
    flags_joined = jnp.concatenate(far_flag_rows, axis=1)
    own_valid = lax.dynamic_slice_in_dim(valid_flags, win_slot * win_dev, win_dev, 0)
    own_factor = band_gain[None, :, None] * own_valid.astype(jnp.float32)[:, None, :]
    own_side = trig_rows(spectra_phase, own_factor)
    cycle_width = offset_count * channels_dev
    own_rows = channels_dev // lax.axis_size(("band", "win"))
    numerator = jnp.einsum("ki,kj->ij", own_side, far_joined, preferred_element_type=jnp.float32)
    counts = jnp.einsum("ki,kj->ij", valid_flags, flags_joined, preferred_element_type=jnp.float32)
    ratio = numerator / jnp.maximum(counts, 1.0)
    crossed = jnp.take_along_axis(ratio[:, cycle_width:], cross_index, axis=1)
    result = lax.psum_scatter(
        jnp.concatenate([ratio[:, :cycle_width], crossed], axis=1),
        ("band", "win"),
        scatter_dimension=0,
        tiled=True,
    )
    coherence = result[:, :cycle_width].reshape(own_rows, offset_count, channels_dev)
    crossing = result[:, cycle_width:]
    return (coherence, crossing)


def solution(mesh):
    placed = (
        P(("groups", "win"), "band", "loop"),
        P("groups", "loop"),
        P("band"),
        P(("groups", "loop"), None),
    )
    return jax.shard_map(
        on_device,
        mesh=mesh,
        in_specs=placed,
        out_specs=(
            P(("groups", "loop", "band", "win"), None, None),
            P(("groups", "loop", "band", "win"), None),
        ),
        check_vma=False,
    )
```

profile of v0, /device:TPU:0, one launch (start us, length us, event | category | flops | bytes accessed | tf_op | source)
XLA Modules:
  0.0 108.5 jit_solution(8983428248087641256)
XLA Ops:
  7.2 0.7 convert_element_type.68
  8.0 1.2 %copy.37 = bf16[2,256,320]{2,1,0:T(8,128)(2,1)S(1)} copy(bf16[2,256,320]{1,2,0:T(8,128)(2,1)} %param.4) | data formatting | bytes 655360 | tf_op args[0]
  9.2 5.1 %collective-permute-start = (bf16[516,320]{1,0:T(8,128)(2,1)S(1)}, bf16[516,320]{1,0:T(8,128)(2,1)}, u32[]{:S(2)}, u32[]{:S(2)}) collective-permute-start(bf16[516,320]{1,0:T(8,128)(2,1)S(1)} %pad_maximum_fusion.5), channel_id=1, source_target_pairs={{0,12},{4,0},{8,4},{12,8},{1,13},{5,1},{9,5},{13,9},{2,14},{6,2},{... | collective-permute-start | bytes 990728 | tf_op jit(solution)/shard_map/ppermute | solution.py:10
  14.4 2.7 %fusion.16 = (bf16[1,2,256,320]{2,3,1,0:T(8,128)(2,1)S(1)}, bf16[1,2,256,320]{2,3,1,0:T(8,128)(2,1)S(1)}, bf16[1,2,256,320]{2,3,1,0:T(8,128)(2,1)S(1)}, bf16[1,2,256,320]{2,3,1,0:T(8,128)(2,1)S(1)}) fusion(bf16[2,256,320]{1,2,0:T(8,128)(2,1)S(1)} %copy-done, f32[2,320]{1,0:T(2,128)S(1)} %dynamic-slice_convert_fusion.2, f32[256]{0:T(256)S(1)} %copy-done.4), kind=kLoop, calls=%fused_computation.36 | loop fusion | flops 1638400 | bytes 1641984 | tf_op jit(solution)/shard_map/stack | solution.py:29
  17.2 0.7 copy.35
  17.9 0.5 convert_element_type.70
  18.4 0.7 copy.36
  19.0 1.3 %convert_element_type.71 = bf16[1024,320]{0,1:T(8,128)(2,1)} reshape(bf16[2,2,256,320]{2,1,0,3:T(2,128)(2,1)S(1)} %copy.36) | data formatting | bytes 1310720 | tf_op jit(solution)/shard_map/convert_element_type | solution.py:30
  20.6 3.4 %collective-permute-done = bf16[516,320]{1,0:T(8,128)(2,1)} collective-permute-done((bf16[516,320]{1,0:T(8,128)(2,1)S(1)}, bf16[516,320]{1,0:T(8,128)(2,1)}, u32[]{:S(2)}, u32[]{:S(2)}) %collective-permute-start) | collective-permute-done | bytes 330272 | tf_op jit(solution)/shard_map/ppermute | solution.py:10
  24.0 3.9 %convert_cosine_fusion.1 = (f32[512,320]{1,0:T(8,128)S(1)}, f32[512,320]{1,0:T(8,128)S(1)}) fusion(bf16[516,320]{1,0:T(8,128)(2,1)} %collective-permute-done), kind=kLoop, calls=%fused_computation.14 | loop fusion | flops 163840 | bytes 1638400 | tf_op jit(solution)/shard_map/cos | solution.py:29
  27.9 0.2 copy.39
  28.1 0.2 copy.41
  28.4 0.7 slice.35
  29.1 10.9 %collective-permute-done.1 = bf16[516,320]{1,0:T(8,128)(2,1)} collective-permute-done((bf16[516,320]{1,0:T(8,128)(2,1)S(1)}, bf16[516,320]{1,0:T(8,128)(2,1)}, u32[]{:S(2)}, u32[]{:S(2)}) %collective-permute-start.1) | collective-permute-done | bytes 330272 | tf_op jit(solution)/shard_map/ppermute | solution.py:16
  39.9 0.7 slice.37
  40.6 0.2 multiply_convert_fusion.3
  40.9 0.7 copy.42
  41.6 1.3 %convert_element_type.74 = bf16[1024,320]{0,1:T(8,128)(2,1)} reshape(bf16[2,2,256,320]{2,1,0,3:T(2,128)(2,1)S(1)} %copy.42) | data formatting | bytes 1310720 | tf_op jit(solution)/shard_map/convert_element_type | solution.py:30
  42.9 3.9 %convert_cosine_fusion = (f32[512,320]{1,0:T(8,128)S(1)}, f32[512,320]{1,0:T(8,128)S(1)}) fusion(bf16[516,320]{1,0:T(8,128)(2,1)} %collective-permute-done.1), kind=kLoop, calls=%fused_computation.12 | loop fusion | flops 163840 | bytes 1638400 | tf_op jit(solution)/shard_map/cos | solution.py:29
  46.8 0.2 copy.44
  47.0 0.2 copy.46
  47.5 0.7 copy.47
  48.2 0.5 convert_element_type.77
  48.8 0.9 fusion
  49.7 0.4 fusion.7
  50.3 20.7 %gather_fusion = f32[2560]{0:T(1024)S(1)} fusion(f32[320,320]{1,0:T(8,128)S(1)} %slice.39, s32[2560]{0:T(1024)S(1)} %reshape.98), kind=kCustom, calls=%fused_computation | custom fusion | bytes 40960 | tf_op jit(solution)/shard_map/jit(take_along_axis)/gather | solution.py:64
  71.4 1.0 pad_maximum_fusion
  72.4 25.9 %reduce-scatter.2.cloned.1.call-done = f32[80,648]{1,0:T(8,128)} async-done(((f32[320,648]{1,0:T(8,128)}), f32[80,648]{1,0:T(8,128)}) %reduce-scatter.2.cloned.1.call-update) | async-done | bytes 207376 | tf_op jit(solution)/shard_map/reduce_scatter | solution.py:65
  98.4 0.9 slice.40
  99.3 0.9 reshape.97
  100.2 0.8 slice.41
  101.0 0.7 copy.51
  (29 shorter events, 1.4 us)
Async XLA Ops:
  7.2 7.2 %copy-start = (bf16[2,256,320]{1,2,0:T(8,128)(2,1)S(1)}, bf16[2,256,320]{1,2,0:T(8,128)(2,1)}, u32[]{:S(2)}) copy-start(bf16[2,256,320]{1,2,0:T(8,128)(2,1)} %param.4) | copy-start | bytes 983044
  7.2 7.2 %copy-start.4 = (f32[256]{0:T(256)S(1)}, f32[256]{0:T(256)}, u32[]{:S(2)}) copy-start(f32[256]{0:T(256)} %param.6) | copy-start | bytes 3076
  7.2 91.2 %reduce-scatter.2.cloned.1.call-start = ((), (), s32[]{:S(2)}) async-start(), calls=%async_computation.1 | async-start | bytes 1228800 | tf_op jit(solution)/shard_map/reduce_scatter | solution.py:65
  9.2 7.9 %copy-start.3 = (s32[320,8]{0,1:T(8,128)S(1)}, s32[320,8]{0,1:T(8,128)}, u32[]{:S(2)}) copy-start(s32[320,8]{0,1:T(8,128)} %param.7) | copy-start | bytes 30724
  9.2 14.8 %collective-permute-start = (bf16[516,320]{1,0:T(8,128)(2,1)S(1)}, bf16[516,320]{1,0:T(8,128)(2,1)}, u32[]{:S(2)}, u32[]{:S(2)}) collective-permute-start(bf16[516,320]{1,0:T(8,128)(2,1)S(1)} %pad_maximum_fusion.5), channel_id=1, source_target_pairs={{0,12},{4,0},{8,4},{12,8},{1,13},{5,1},{9,5},{13,9},{2,14},{6,2},{... | collective-permute-start | bytes 990728 | tf_op jit(solution)/shard_map/ppermute | solution.py:10
  14.3 25.6 %collective-permute-start.1 = (bf16[516,320]{1,0:T(8,128)(2,1)S(1)}, bf16[516,320]{1,0:T(8,128)(2,1)}, u32[]{:S(2)}, u32[]{:S(2)}) collective-permute-start(bf16[516,320]{1,0:T(8,128)(2,1)S(1)} %pad_maximum_fusion.5), channel_id=1, source_target_pairs={{0,8},{4,12},{8,0},{12,4},{1,9},{5,13},{9,1},{13,5},{2,10},{6,14},... | collective-permute-start | bytes 990728 | tf_op jit(solution)/shard_map/ppermute | solution.py:16
  47.5 1.2 %copy-start.1 = (bf16[1024,320]{0,1:T(8,128)(2,1)S(1)}, bf16[1024,320]{0,1:T(8,128)(2,1)}, u32[]{:S(2)}) copy-start(bf16[1024,320]{0,1:T(8,128)(2,1)} %convert_element_type.71) | copy-start | bytes 1966084
  47.5 1.3 %copy-start.2 = (bf16[1024,320]{0,1:T(8,128)(2,1)S(1)}, bf16[1024,320]{0,1:T(8,128)(2,1)}, u32[]{:S(2)}) copy-start(bf16[1024,320]{0,1:T(8,128)(2,1)} %convert_element_type.74) | copy-start | bytes 1966084
Sparse Core Ops, SparseCore 0:
  72.6 25.7 reduce-scatter.1
where the time goes:
time: 109 us
  waiting for transfers between devices  40.2 us (37%)
  local copies, waits for them, and re-layouts  34.7 us (32%)
  between operations  14.3 us (13%)
  other arithmetic  12.9 us (12%)
  starting transfers between devices  5.14 us (5%)
  matrix products  1.31 us (1%)
    reduce_scatter x1, waiting for transfers between devices, on_device(): lax.psum_scatter(jnp.concatenate([ratio[:, :cycle_width], crossed], axis=...  25.9 us
    gather x5, local copies, waits for them, and re-layouts, on_device(): crossed = jnp.take_along_axis(ratio[:, cycle_width:], cross_index, axis=1)  21.2 us
    ppermute x1, waiting for transfers between devices, swapped(): return lax.ppermute(value, axis, pairs)  10.9 us
    cos x2, other arithmetic, trig_rows(): stacked = jnp.stack([jnp.cos(values) * factor, jnp.sin(values) * factor])  7.8 us
    ppermute x1, starting transfers between devices, passed_along(): return lax.ppermute(value, axis, pairs)  5.1 us
    convert_element_type x4, local copies, waits for them, and re-layouts, trig_rows(): return stacked.astype(jnp.bfloat16).reshape(-1, phases.shape[-1])  3.55 us
    ppermute x1, waiting for transfers between devices, passed_along(): return lax.ppermute(value, axis, pairs)  3.36 us
    another operation x4, other arithmetic, trig_rows(): stacked = jnp.stack([jnp.cos(values) * factor, jnp.sin(values) * factor])  2.95 us
  transfers between devices with their start and end apart: 3, of which 3 were waited for; matrix products, arithmetic and copies ran while one was open for 10% of the time, Pallas kernels for 0%

commit v1 on v0

v1 whole, which is shorter than its diff:
```python
import functools
import math

import jax
import jax.numpy as jnp
from jax import lax
from jax.experimental import pallas as pl
from jax.experimental.pallas import tpu as pltpu
from jax.sharding import PartitionSpec as P

MESH = pl.DeviceIdType.MESH
SIN = (0.9999995827674866, -0.16666549444198608, 0.008332383818924427,
       -0.00019808131037279963, 2.6991506274498533e-06, -2.033945278867577e-08)
COS = (1.0, -0.49999988079071045, 0.041666485369205475, -0.0013887780951336026,
       2.4769393348833546e-05, -2.707419355374441e-07, 1.7227314019763185e-09)
FLAG_ROWS = 8


def horner(coefficients, u):
    total = coefficients[-1] * u + coefficients[-2]
    for c in coefficients[-3::-1]:
        total = total * u + c
    return total


def cos_sin(x):
    u = x * x
    return horner(COS, u), horner(SIN, u) * x


def dot_t(a, b):
    return lax.dot_general(a, b, (((1,), (1,)), ((), ())), preferred_element_type=jnp.float32)


def row_dot(a, b):
    return lax.dot_general(a, b, (((1,), (0,)), ((), ())), preferred_element_type=jnp.float32)


def kernel(
    plan, phase_ref, valid_ref, gain_ref, index_ref, coh_ref, cross_ref,
    phase, far_phase, own_flags, far_flags, turn, columns, own_side, far_side,
    part, part_in, xpart, xpart_in,
    load_sem, flag_send, flag_recv, loop_send, loop_recv, sum_send, sum_recv,
):
    n_loop, n_band, n_win, offsets, chunk = plan
    wins, channels, freq = phase.shape
    cycles = part.shape[0]
    owners = n_band * n_win
    own_rows = channels // owners
    windows = valid_ref.shape[0]
    far_slots = len(offsets)
    loop_at = lax.axis_index("loop")
    win_at = lax.axis_index("win")
    owner_at = lax.axis_index("band") * n_win + win_at

    def loop_device(steps):
        return {"loop": lax.rem(loop_at + (steps % n_loop), n_loop)}

    def owner_of(d):
        return lax.rem(owner_at + d, owners)

    def owner_device(d):
        owner = owner_of(d)
        return {"band": owner // n_win, "win": lax.rem(owner, n_win)}

    barrier = pltpu.get_barrier_semaphore()
    greeted = sorted({o % n_loop for o in offsets} | {-o % n_loop for o in offsets})
    for steps in greeted:
        pl.semaphore_signal(barrier, inc=1, device_id=loop_device(steps), device_id_type=MESH)
    for d in range(1, owners):
        pl.semaphore_signal(barrier, inc=1, device_id=owner_device(d), device_id_type=MESH)
    loads = [
        pltpu.make_async_copy(phase_ref.at[w], phase.at[w], load_sem.at[w]) for w in range(wins)
    ]
    for load in loads:
        load.start()
    own_flags[...] = jnp.zeros_like(own_flags)
    own_flags[0:windows, :] = valid_ref[...].astype(jnp.float32)
    pl.semaphore_wait(barrier, len(greeted) + owners - 1)

    flag_copies, loop_copies = [], []
    for p, offset in enumerate(offsets):
        copy = pltpu.make_async_remote_copy(
            own_flags, far_flags.at[p], flag_send.at[p], flag_recv.at[p],
            device_id=loop_device(-offset), device_id_type=MESH,
        )
        copy.start()
        flag_copies.append(copy)
    for p, offset in enumerate(offsets):
        copies = []
        for w in range(wins):
            copy = pltpu.make_async_remote_copy(
                phase_ref.at[w], far_phase.at[p, w], loop_send.at[p, w], loop_recv.at[p, w],
                device_id=loop_device(-offset), device_id_type=MESH,
            )
            copy.start()
            copies.append(copy)
        loop_copies.append(copies)

    def window_row(flags_ref, w):
        return flags_ref[pl.ds(win_at * wins + w, 1), :]

    def turned(flags_ref, slot):
        turn[...] = jnp.zeros_like(turn)
        turn[0:FLAG_ROWS, 0:channels] = flags_ref[...]
        for w in range(wins):
            turn[FLAG_ROWS + w : FLAG_ROWS + w + 1, 0:channels] = window_row(flags_ref, w)
        columns[slot] = jnp.transpose(turn[...])[0:channels, :]

    def column(slot, w):
        return columns[slot, :, FLAG_ROWS + w : FLAG_ROWS + w + 1]

    def inverse_counts(slot, flags_ref):
        counts = row_dot(columns[slot, :, 0:FLAG_ROWS], flags_ref[...])
        return 1.0 / jnp.maximum(counts, 1.0)

    def far_trig(source, w):
        def step(c, _):
            rows = pl.ds(pl.multiple_of(c * chunk, chunk), chunk)
            cosine, sine = cos_sin(source[rows, :].astype(jnp.float32))
            far_side[w, rows, 0:freq] = cosine.astype(jnp.bfloat16)
            far_side[w, rows, freq : 2 * freq] = sine.astype(jnp.bfloat16)
            return 0

        lax.fori_loop(0, channels // chunk, step, 0)

    turned(own_flags, 0)
    gain = gain_ref[...]

    def own_trig(w):
        def step(c, _):
            rows = pl.ds(pl.multiple_of(c * chunk, chunk), chunk)
            cosine, sine = cos_sin(phase[w, rows, :].astype(jnp.float32))
            far_side[w, rows, 0:freq] = cosine.astype(jnp.bfloat16)
            far_side[w, rows, freq : 2 * freq] = sine.astype(jnp.bfloat16)
            factor = gain * columns[0, rows, FLAG_ROWS + w : FLAG_ROWS + w + 1]
            own_side[w, rows, 0:freq] = (cosine * factor).astype(jnp.bfloat16)
            own_side[w, rows, freq : 2 * freq] = (sine * factor).astype(jnp.bfloat16)
            return 0

        lax.fori_loop(0, channels // chunk, step, 0)

    sums = []

    def send_sum(piece, source, target, d):
        copy = pltpu.make_async_remote_copy(
            source.at[owner_of(d)], target.at[d - 1],
            sum_send.at[piece, d - 1], sum_recv.at[piece, d - 1],
            device_id=owner_device(d), device_id_type=MESH,
        )
        copy.start()
        sums.append(copy)

    def coherence_piece(k, flags_ref):
        ratio = dot_t(own_side[0], far_side[0]) * window_row(flags_ref, 0)
        for w in range(1, wins):
            ratio += dot_t(own_side[w], far_side[w]) * window_row(flags_ref, w)
        ratio = ratio * inverse_counts(0, flags_ref)
        for r in range(owners):
            part[k, r] = ratio[r * own_rows : (r + 1) * own_rows, :].astype(jnp.bfloat16)
        for d in range(1, owners):
            send_sum(k, part.at[k], part_in.at[k], d)

    for w in range(wins):
        loads[w].wait()
        own_trig(w)
    coherence_piece(0, own_flags)

    for p in range(far_slots):
        flags_ref = far_flags.at[p]
        flag_copies[p].wait_recv()
        if p == far_slots - 1:
            turned(flags_ref, 1)
        for w in range(wins):
            loop_copies[p][w].wait_recv()
            far_trig(far_phase.at[p, w], w)
        if p < far_slots - 1:
            coherence_piece(p + 1, flags_ref)
        else:
            ratio = dot_t(far_side[0], own_side[0]) * column(1, 0)
            for w in range(1, wins):
                ratio += dot_t(far_side[w], own_side[w]) * column(1, w)
            ratio = ratio * inverse_counts(1, own_flags)
            position = lax.broadcasted_iota(jnp.int32, ratio.shape, 0)
            near = index_ref.shape[0]
            chosen = jnp.concatenate(
                [
                    jnp.sum(
                        jnp.where(position == index_ref[n : n + 1, :], ratio, 0.0),
                        axis=0, keepdims=True,
                    )
                    for n in range(near)
                ],
                axis=0,
            )
            for r in range(owners):
                xpart[r, :, 0:own_rows] = chosen[:, r * own_rows : (r + 1) * own_rows]
            for d in range(1, owners):
                send_sum(cycles, xpart, xpart_in, d)

    for k in range(cycles):
        total = part[k, owner_at].astype(jnp.float32)
        for d in range(1, owners):
            sums[k * (owners - 1) + d - 1].wait_recv()
            total += part_in[k, d - 1].astype(jnp.float32)
        coh_ref[:, k, :] = total
    total = xpart[owner_at]
    for d in range(1, owners):
        sums[cycles * (owners - 1) + d - 1].wait_recv()
        total += xpart_in[d - 1]
    cross_ref[...] = total[:, 0:own_rows]

    for copy in flag_copies:
        copy.wait_send()
    for copies in loop_copies:
        for copy in copies:
            copy.wait_send()
    for copy in sums:
        copy.wait_send()


def on_device(spectra_phase, window_valid, band_gain, cross_index):
    wins, freq, channels = spectra_phase.shape
    windows = window_valid.shape[0]
    near = cross_index.shape[1]
    n_loop = lax.axis_size("loop")
    n_band = lax.axis_size("band")
    n_win = lax.axis_size("win")
    owners = n_band * n_win
    own_rows = channels // owners
    far_reach = n_loop // 4
    offsets = tuple(range(1, far_reach + 1)) + (n_loop // 2,)
    cycles = far_reach + 1
    slots = len(offsets)
    chunk = math.gcd(channels, 32)
    lanes = -(-own_rows // 128) * 128
    wide = -(-channels // 128) * 128
    vmem = pl.BlockSpec(memory_space=pltpu.VMEM)
    coherence, crossing = pl.pallas_call(
        functools.partial(kernel, (n_loop, n_band, n_win, offsets, chunk)),
        out_shape=(
            jax.ShapeDtypeStruct((own_rows, cycles, channels), jnp.float32),
            jax.ShapeDtypeStruct((near, own_rows), jnp.float32),
        ),
        in_specs=[pl.BlockSpec(memory_space=pl.ANY), vmem, vmem, vmem],
        out_specs=(vmem, vmem),
        scratch_shapes=[
            pltpu.VMEM((wins, channels, freq), jnp.bfloat16),
            pltpu.VMEM((slots, wins, channels, freq), jnp.bfloat16),
            pltpu.VMEM((FLAG_ROWS, channels), jnp.float32),
            pltpu.VMEM((slots, FLAG_ROWS, channels), jnp.float32),
            pltpu.VMEM((128, wide), jnp.float32),
            pltpu.VMEM((2, channels, 128), jnp.float32),
            pltpu.VMEM((wins, channels, 2 * freq), jnp.bfloat16),
            pltpu.VMEM((wins, channels, 2 * freq), jnp.bfloat16),
            pltpu.VMEM((cycles, owners, own_rows, channels), jnp.bfloat16),
            pltpu.VMEM((cycles, owners - 1, own_rows, channels), jnp.bfloat16),
            pltpu.VMEM((owners, near, lanes), jnp.float32),
            pltpu.VMEM((owners - 1, near, lanes), jnp.float32),
            pltpu.SemaphoreType.DMA((wins,)),
            pltpu.SemaphoreType.DMA((slots,)),
            pltpu.SemaphoreType.DMA((slots,)),
            pltpu.SemaphoreType.DMA((slots, wins)),
            pltpu.SemaphoreType.DMA((slots, wins)),
            pltpu.SemaphoreType.DMA((cycles + 1, owners - 1)),
            pltpu.SemaphoreType.DMA((cycles + 1, owners - 1)),
        ],
        compiler_params=pltpu.CompilerParams(
            collective_id=0, has_side_effects=True, vmem_limit_bytes=48 * 1024 * 1024
        ),
        name="coherence",
    )(
        jnp.swapaxes(spectra_phase, 1, 2),
        window_valid,
        band_gain.reshape(1, freq),
        cross_index.T,
    )
    return coherence, crossing.T


def solution(mesh):
    placed = (
        P(("groups", "win"), "band", "loop"),
        P("groups", "loop"),
        P("band"),
        P(("groups", "loop"), None),
    )
    return jax.shard_map(
        on_device,
        mesh=mesh,
        in_specs=placed,
        out_specs=(
            P(("groups", "loop", "band", "win"), None, None),
            P(("groups", "loop", "band", "win"), None),
        ),
        check_vma=False,
    )
```

time: 109 us -> 38.1 us (0.35)
  waiting for transfers between devices: 40.2 us -> 0 us
  Pallas kernels: 0 us -> 32.8 us
  local copies, waits for them, and re-layouts: 34.7 us -> 4.33 us
  between operations: 14.3 us -> 0.65 us
  other arithmetic: 12.9 us -> 0 us
  starting transfers between devices: 5.14 us -> 0 us
  matrix products: 1.31 us -> 0 us
    pallas_call x0 -> x1, Pallas kernels: none -> 32.8 us  [on_device(): pl.pallas_call(functools.partial(kernel, (n_loop, n_band, n_win, offsets,...]
    reduce_scatter x1 -> x0, waiting for transfers between devices: 25.9 us -> none  [on_device(): lax.psum_scatter(jnp.concatenate([ratio[:, :cycle_width], crossed], axis=...]
    gather x5 -> x0, local copies, waits for them, and re-layouts: 21.2 us -> none  [on_device(): crossed = jnp.take_along_axis(ratio[:, cycle_width:], cross_index, axis=1)]
    ppermute x2 -> x0, waiting for transfers between devices: 14.2 us -> none  [the longest x1 10.9 us: swapped(): return lax.ppermute(value, axis, pairs)]
    cos x2 -> x0, other arithmetic: 7.8 us -> none  [trig_rows(): stacked = jnp.stack([jnp.cos(values) * factor, jnp.sin(values) * factor])]
    ppermute x2 -> x0, starting transfers between devices: 5.1 us -> none  [the longest x1 5.1 us: passed_along(): return lax.ppermute(value, axis, pairs)]
    convert_element_type x4 -> x0, local copies, waits for them, and re-layouts: 3.55 us -> none  [trig_rows(): return stacked.astype(jnp.bfloat16).reshape(-1, phases.shape[-1])]
    another operation x6 -> x0, other arithmetic: 3.25 us -> none  [the longest x4 2.95 us: trig_rows(): stacked = jnp.stack([jnp.cos(values) * factor, jnp.sin(values) * factor])]
  transfers between devices with their start and end apart: 3 -> 0, of which waited for: 3 -> 0; matrix products, arithmetic and copies ran while one was open for 10% -> 0% of each run, Pallas kernels for 0% -> 0%
where the time goes in v1:
time: 38.1 us; the launch traced here: 37.8 us
  Pallas kernels  32.8 us (86%)
  local copies, waits for them, and re-layouts  4.33 us (11%)
  between operations  0.65 us (2%)
    pallas_call x1, Pallas kernels, on_device(): pl.pallas_call(functools.partial(kernel, (n_loop, n_band, n_win, offsets,...  32.8 us
    unnamed x10, local copies, waits for them, and re-layouts  4.33 us

profile of v1, /device:TPU:0, one launch (start us, length us, event | category | flops | bytes accessed | tf_op | source)
XLA Modules:
  0.0 37.8 jit_solution(9728667965925636771)
XLA Ops:
  0.6 0.0 copy-start.3
  0.6 0.7 %copy-done.3 = f32[256]{0:T(256)S(1)} copy-done((f32[256]{0:T(256)S(1)}, f32[256]{0:T(256)}, u32[]{:S(2)}) %copy-start.3) | copy-done | bytes 1048
  1.3 0.0 copy-start
  1.3 1.0 %copy-done = bf16[2,256,320]{1,2,0:T(8,128)(2,1)S(1)} copy-done((bf16[2,256,320]{1,2,0:T(8,128)(2,1)S(1)}, bf16[2,256,320]{1,2,0:T(8,128)(2,1)}, u32[]{:S(2)}) %copy-start) | copy-done | bytes 327704
  2.3 0.0 copy-start.1
  2.3 0.7 %copy-done.1 = s32[320,8]{0,1:T(8,128)S(1)} copy-done((s32[320,8]{0,1:T(8,128)S(1)}, s32[320,8]{0,1:T(8,128)}, u32[]{:S(2)}) %copy-start.1) | copy-done | bytes 10264
  3.0 0.0 copy-start.2
  3.0 0.7 %copy-done.2 = s32[4,320]{1,0:T(4,128)S(1)} copy-done((s32[4,320]{1,0:T(4,128)S(1)}, s32[4,320]{1,0:T(4,128)}, u32[]{:S(2)}) %copy-start.2) | copy-done | bytes 5144
  3.7 32.8 %coherence.1 = (f32[80,2,320]{2,1,0:T(2,128)S(1)}, f32[8,80]{1,0:T(8,128)S(1)}) custom-call(bf16[2,320,256]{2,1,0:T(8,128)(2,1)S(1)} %bitcast.4, s32[4,320]{1,0:T(4,128)S(1)} %copy-done.2, f32[1,256]{1,0:T(1,128)S(1)} %bitcast.7, s32[8,320]{1,0:T(8,128)S(1)} %bitcast.5), custom_call_target="tpu_custom_call" | custom-call | tf_op jit(solution)/shard_map/coherence/pallas_call | solution.py:239
  36.5 0.7 %copy.8 = f32[80,2,320]{2,1,0:T(2,128)} copy(f32[80,2,320]{2,1,0:T(2,128)S(1)} %get-tuple-element.8) | data formatting | bytes 409600
  37.2 0.6 %copy.9 = f32[80,8]{0,1:T(8,128)} copy(f32[80,8]{0,1:T(8,128)S(1)} %bitcast.6) | data formatting | bytes 5120
Async XLA Ops:
  0.6 0.7 %copy-start.3 = (f32[256]{0:T(256)S(1)}, f32[256]{0:T(256)}, u32[]{:S(2)}) copy-start(f32[256]{0:T(256)} %param.6) | copy-start | bytes 3076
  1.3 1.0 %copy-start = (bf16[2,256,320]{1,2,0:T(8,128)(2,1)S(1)}, bf16[2,256,320]{1,2,0:T(8,128)(2,1)}, u32[]{:S(2)}) copy-start(bf16[2,256,320]{1,2,0:T(8,128)(2,1)} %param.4) | copy-start | bytes 983044
  2.3 0.7 %copy-start.1 = (s32[320,8]{0,1:T(8,128)S(1)}, s32[320,8]{0,1:T(8,128)}, u32[]{:S(2)}) copy-start(s32[320,8]{0,1:T(8,128)} %param.7) | copy-start | bytes 30724
  3.0 0.7 %copy-start.2 = (s32[4,320]{1,0:T(4,128)S(1)}, s32[4,320]{1,0:T(4,128)}, u32[]{:S(2)}) copy-start(s32[4,320]{1,0:T(4,128)} %valid_ref.1) | copy-start | bytes 15364

commit v2 on v1

--- a/solution.py
+++ b/solution.py
@@ -219,6 +219,334 @@
         copy.wait_send()
 
 
+NEXT, OPPOSITE = 0, 1
+ARRIVALS = (
+    ((NEXT, 0), (NEXT, 1), (NEXT, 2), (NEXT, 3)),
+    ((NEXT, 0), (NEXT, 1), (OPPOSITE, 2), (NEXT, 2), (OPPOSITE, 3), (NEXT, 3)),
+    ((OPPOSITE, 0), (NEXT, 2), (OPPOSITE, 1), (NEXT, 3),
+     (OPPOSITE, 2), (NEXT, 0), (OPPOSITE, 3), (NEXT, 1)),
+    ((OPPOSITE, 0), (OPPOSITE, 1), (NEXT, 0), (NEXT, 1), (NEXT, 2), (NEXT, 3)),
+)
+OWN_SENDS = (
+    ((2, OPPOSITE, 0), (2, OPPOSITE, 1), (2, OPPOSITE, 2), (2, OPPOSITE, 3)),
+    ((3, OPPOSITE, 0), (0, NEXT, 0), (3, OPPOSITE, 1), (0, NEXT, 1), (0, NEXT, 2), (0, NEXT, 3)),
+    ((1, NEXT, 0), (1, NEXT, 1), (1, NEXT, 2), (1, NEXT, 3)),
+    ((2, NEXT, 2), (2, NEXT, 3), (2, NEXT, 0), (2, NEXT, 1)),
+)
+RELAYS = {
+    (OPPOSITE, 0): (3, NEXT), (OPPOSITE, 1): (3, NEXT),
+    (OPPOSITE, 2): (3, NEXT), (OPPOSITE, 3): (3, NEXT),
+    (NEXT, 2): (1, OPPOSITE), (NEXT, 3): (1, OPPOSITE),
+}
+PAIR_WINDOWS = ((), (1,), (0, 1), (0,))
+
+
+def kernel_of_four(
+    plan, phase_ref, valid_ref, gain_ref, index_ref, coh_ref, cross_ref,
+    phase, gain, index, valid, far_phase, flags, turn, columns,
+    own_side, far_own, far_next, own_opposite, far_opposite, inverse,
+    part, part_in, xpart, xpart_in, xopposite_in,
+    load_sem, small_send, small_recv, own_send, relay_send, recv,
+    sum_send, sum_recv, xsend, xrecv, ysend, yrecv,
+):
+    n_band, n_win, chunk = plan
+    wins, channels, freq = phase.shape
+    owners = n_band * n_win
+    own_rows = channels // owners
+    windows = valid_ref.shape[0]
+    near = index_ref.shape[0]
+    half = channels // 2
+    at = lax.axis_index("loop")
+    win_at = lax.axis_index("win")
+    owner_at = lax.axis_index("band") * n_win + win_at
+    across = lax.rem(at + 2, 4)
+    before = lax.rem(at + 3, 4)
+
+    def owner_of(d):
+        return lax.rem(owner_at + d, owners)
+
+    def owner_device(d, position=None):
+        owner = owner_of(d)
+        place = {"band": owner // n_win, "win": lax.rem(owner, n_win)}
+        if position is not None:
+            place["loop"] = position
+        return place
+
+    def remote(source, target, send_sem, recv_sem, device):
+        return pltpu.make_async_remote_copy(
+            source, target, send_sem, recv_sem, device_id=device, device_id_type=MESH
+        )
+
+    loads = [
+        pltpu.make_async_copy(valid_ref, valid.at[0], load_sem.at[0]),
+        pltpu.make_async_copy(gain_ref, gain, load_sem.at[1]),
+        pltpu.make_async_copy(index_ref, index.at[0], load_sem.at[2]),
+    ]
+    for w in range(wins):
+        loads.append(pltpu.make_async_copy(phase_ref.at[w], phase.at[w], load_sem.at[3 + w]))
+    for load in loads:
+        load.start()
+    barrier = pltpu.get_barrier_semaphore()
+    for steps in (1, 2, 3):
+        pl.semaphore_signal(
+            barrier, inc=1, device_id={"loop": lax.rem(at + steps, 4)}, device_id_type=MESH
+        )
+    for d in range(1, owners):
+        for position in (None, across):
+            pl.semaphore_signal(
+                barrier, inc=1, device_id=owner_device(d, position), device_id_type=MESH
+            )
+    turn[...] = jnp.zeros_like(turn)
+    flags[...] = jnp.zeros_like(flags)
+    pl.semaphore_wait(barrier, 3 + 2 * (owners - 1))
+
+    smalls = [
+        remote(valid_ref, valid.at[1], small_send.at[0], small_recv.at[0], {"loop": before}),
+        remote(valid_ref, valid.at[2], small_send.at[1], small_recv.at[1], {"loop": across}),
+        remote(index_ref, index.at[1], small_send.at[2], small_recv.at[2], {"loop": across}),
+    ]
+    for copy in smalls:
+        copy.start()
+
+    def quarter(ref, q):
+        return ref.at[q // 2, pl.ds((q % 2) * half, half)]
+
+    def own_copies(z):
+        return [
+            remote(
+                quarter(phase_ref, q), quarter(far_phase.at[slot], q),
+                own_send.at[n], recv.at[slot, q], {"loop": target},
+            )
+            for n, (target, slot, q) in enumerate(OWN_SENDS[z])
+        ]
+
+    for z in range(4):
+        @pl.when(at == z)
+        def _():
+            for copy in own_copies(z):
+                copy.start()
+
+    def window_row(slot, w):
+        return flags[slot, pl.ds(win_at * wins + w, 1), :]
+
+    def turned(flag_slot, slot):
+        turn[0:FLAG_ROWS, 0:channels] = flags[flag_slot]
+        for w in range(wins):
+            turn[FLAG_ROWS + w : FLAG_ROWS + w + 1, 0:channels] = window_row(flag_slot, w)
+        columns[slot] = jnp.transpose(turn[...])[0:channels, :]
+
+    def column(slot, w):
+        return columns[slot, :, FLAG_ROWS + w : FLAG_ROWS + w + 1]
+
+    def inverse_counts(slot, flag_slot):
+        counts = row_dot(columns[slot, :, 0:FLAG_ROWS], flags[flag_slot])
+        return 1.0 / jnp.maximum(counts, 1.0)
+
+    def trig(source, far, own, column_slot, q):
+        w = q // 2
+        gains = gain[...]
+
+        def step(c, _):
+            rows = pl.ds(pl.multiple_of((q % 2) * half + c * chunk, chunk), chunk)
+            cosine, sine = cos_sin(source[w, rows, :].astype(jnp.float32))
+            far[w, rows, 0:freq] = cosine.astype(jnp.bfloat16)
+            far[w, rows, freq : 2 * freq] = sine.astype(jnp.bfloat16)
+            if own is not None:
+                factor = gains * columns[column_slot, rows, FLAG_ROWS + w : FLAG_ROWS + w + 1]
+                own[w, rows, 0:freq] = (cosine * factor).astype(jnp.bfloat16)
+                own[w, rows, freq : 2 * freq] = (sine * factor).astype(jnp.bfloat16)
+            return 0
+
+        lax.fori_loop(0, half // chunk, step, 0)
+
+    sums = []
+
+    def coherence_piece(k, far, scale):
+        ratio = dot_t(own_side[0], far[0]) * window_row(k, 0)
+        for w in range(1, wins):
+            ratio += dot_t(own_side[w], far[w]) * window_row(k, w)
+        ratio = ratio * scale
+        for r in range(owners):
+            part[k, r] = ratio[r * own_rows : (r + 1) * own_rows, :].astype(jnp.bfloat16)
+        for d in range(1, owners):
+            copy = remote(
+                part.at[k, owner_of(d)], part_in.at[k, d - 1],
+                sum_send.at[k, d - 1], sum_recv.at[k, d - 1], owner_device(d),
+            )
+            copy.start()
+            sums.append(copy)
+
+    def own_xcopies():
+        return [
+            remote(
+                xpart.at[0, owner_of(d)], xpart_in.at[d - 1],
+                xsend.at[d - 1], xrecv.at[d - 1], owner_device(d),
+            )
+            for d in range(1, owners)
+        ]
+
+    def opposite_xcopies():
+        return [
+            remote(
+                xpart.at[1, owner_of(d)], xopposite_in.at[d],
+                ysend.at[d], yrecv.at[d], owner_device(d, across),
+            )
+            for d in range(owners)
+        ]
+
+    def crossing_piece(side, far, own, column_slot, pair_windows):
+        ratio = None
+        for w in pair_windows:
+            term = dot_t(far[w], own[w]) * column(column_slot, w)
+            ratio = term if ratio is None else ratio + term
+        ratio = ratio * inverse[1 + side]
+        position = lax.broadcasted_iota(jnp.int32, ratio.shape, 0)
+        rows = []
+        for n in range(near):
+            hit = position == index[side, n : n + 1, :]
+            rows.append(jnp.sum(jnp.where(hit, ratio, 0.0), axis=0, keepdims=True))
+        chosen = jnp.concatenate(rows, axis=0)
+        for r in range(owners):
+            xpart[side, r, :, 0:own_rows] = chosen[:, r * own_rows : (r + 1) * own_rows]
+
+    for load in loads[:3]:
+        load.wait()
+    flags[0, 0:windows, :] = valid[0].astype(jnp.float32)
+    turned(0, 0)
+    for w in range(wins):
+        loads[3 + w].wait()
+        for q in (2 * w, 2 * w + 1):
+            trig(phase, far_own, own_side, 0, q)
+    coherence_piece(0, far_own, inverse_counts(0, 0))
+
+    for copy in smalls:
+        copy.wait_recv()
+    flags[1, 0:windows, :] = valid[1].astype(jnp.float32)
+    flags[2, 0:windows, :] = valid[2].astype(jnp.float32)
+    turned(2, 1)
+    inverse[0] = inverse_counts(0, 1)
+    inverse[1] = inverse_counts(1, 0)
+    inverse[2] = inverse_counts(0, 2)
+
+    def relay_copies():
+        copies = {}
+        for n, ((slot, q), (target, there)) in enumerate(sorted(RELAYS.items())):
+            copies[slot, q] = remote(
+                quarter(far_phase.at[slot], q), quarter(far_phase.at[there], q),
+                relay_send.at[n], recv.at[there, q], {"loop": target},
+            )
+        return copies
+
+    for z in range(4):
+        @pl.when(at == z)
+        def _():
+            relays = relay_copies() if z == 2 else {}
+            for slot, q in ARRIVALS[z]:
+                landed = quarter(far_phase.at[slot], q)
+                remote(
+                    landed, landed, relay_send.at[0], recv.at[slot, q], {"loop": (z + 1) % 4}
+                ).wait_recv()
+                if (slot, q) in relays:
+                    relays[slot, q].start()
+                if slot == NEXT:
+                    trig(far_phase.at[NEXT], far_next, None, None, q)
+                else:
+                    trig(far_phase.at[OPPOSITE], far_opposite, own_opposite, 1, q)
+
+    coherence_piece(1, far_next, inverse[0])
+    for z in range(1, 4):
+        @pl.when(at == z)
+        def _():
+            crossing_piece(1, far_own, own_opposite, 0, PAIR_WINDOWS[z])
+            for copy in opposite_xcopies():
+                copy.start()
+            crossing_piece(0, far_opposite, own_side, 1, PAIR_WINDOWS[z])
+            for copy in own_xcopies():
+                copy.start()
+
+    for k in range(2):
+        total = part[k, owner_at].astype(jnp.float32)
+        for d in range(1, owners):
+            sums[k * (owners - 1) + d - 1].wait_recv()
+            total += part_in[k, d - 1].astype(jnp.float32)
+        coh_ref[:, k, :] = total
+
+    for z in range(4):
+        @pl.when(at == z)
+        def _():
+            total = jnp.zeros((near, xpart.shape[-1]), jnp.float32)
+            if z != 0:
+                total += xpart[0, owner_at]
+                for d, copy in enumerate(own_xcopies()):
+                    copy.wait_recv()
+                    total += xpart_in[d]
+            if z != 2:
+                for d, copy in enumerate(opposite_xcopies()):
+                    copy.wait_recv()
+                    total += xopposite_in[d]
+            cross_ref[...] = total[:, 0:own_rows]
+            for copy in own_copies(z):
+                copy.wait_send()
+            if z == 2:
+                for copy in relay_copies().values():
+                    copy.wait_send()
+            if z != 0:
+                for copy in own_xcopies() + opposite_xcopies():
+                    copy.wait_send()
+
+    for copy in smalls:
+        copy.wait_send()
+    for copy in sums:
+        copy.wait_send()
+
+
+def call_of_four(phases, valid, gain, index, n_band, n_win):
+    wins, channels, freq = phases.shape
+    windows, near = valid.shape[0], index.shape[0]
+    owners = n_band * n_win
+    own_rows = channels // owners
+    chunk = math.gcd(channels // 2, 32)
+    lanes = -(-own_rows // 128) * 128
+    wide = -(-channels // 128) * 128
+    vmem = pl.BlockSpec(memory_space=pltpu.VMEM)
+    hbm = pl.BlockSpec(memory_space=pltpu.HBM)
+    sides = pltpu.VMEM((wins, channels, 2 * freq), jnp.bfloat16)
+    dma = pltpu.SemaphoreType.DMA
+    return pl.pallas_call(
+        functools.partial(kernel_of_four, (n_band, n_win, chunk)),
+        out_shape=(
+            jax.ShapeDtypeStruct((own_rows, 2, channels), jnp.float32),
+            jax.ShapeDtypeStruct((near, own_rows), jnp.float32),
+        ),
+        in_specs=[hbm, hbm, hbm, hbm],
+        out_specs=(vmem, vmem),
+        scratch_shapes=[
+            pltpu.VMEM((wins, channels, freq), jnp.bfloat16),
+            pltpu.VMEM((1, freq), jnp.float32),
+            pltpu.VMEM((2, near, channels), jnp.int32),
+            pltpu.VMEM((3, windows, channels), jnp.int32),
+            pltpu.VMEM((2, wins, channels, freq), jnp.bfloat16),
+            pltpu.VMEM((3, FLAG_ROWS, channels), jnp.float32),
+            pltpu.VMEM((128, wide), jnp.float32),
+            pltpu.VMEM((2, channels, 128), jnp.float32),
+            sides, sides, sides, sides, sides,
+            pltpu.VMEM((3, channels, channels), jnp.float32),
+            pltpu.VMEM((2, owners, own_rows, channels), jnp.bfloat16),
+            pltpu.VMEM((2, owners - 1, own_rows, channels), jnp.bfloat16),
+            pltpu.VMEM((2, owners, near, lanes), jnp.float32),
+            pltpu.VMEM((owners - 1, near, lanes), jnp.float32),
+            pltpu.VMEM((owners, near, lanes), jnp.float32),
+            dma((3 + wins,)), dma((3,)), dma((3,)), dma((6,)), dma((6,)), dma((2, 4)),
+            dma((2, owners - 1)), dma((2, owners - 1)),
+            dma((owners - 1,)), dma((owners - 1,)), dma((owners,)), dma((owners,)),
+        ],
+        compiler_params=pltpu.CompilerParams(
+            collective_id=1, has_side_effects=True, vmem_limit_bytes=48 * 1024 * 1024
+        ),
+        name="coherence_of_four",
+    )(phases, valid, gain, index)
+
+
 def on_device(spectra_phase, window_valid, band_gain, cross_index):
     wins, freq, channels = spectra_phase.shape
     windows = window_valid.shape[0]
@@ -228,6 +556,12 @@
     n_win = lax.axis_size("win")
     owners = n_band * n_win
     own_rows = channels // owners
+    if n_loop == 4 and wins == 2 and owners > 1:
+        coherence, crossing = call_of_four(
+            jnp.swapaxes(spectra_phase, 1, 2), window_valid,
+            band_gain.reshape(1, freq), cross_index.T, n_band, n_win,
+        )
+        return coherence, crossing.T
     far_reach = n_loop // 4
     offsets = tuple(range(1, far_reach + 1)) + (n_loop // 2,)
     cycles = far_reach + 1

time: 38.1 us -> 32.5 us (0.85)
  the two profiles are of different devices: /device:TPU:0 before, /device:TPU:11 now
where the time goes in v2:
time: 32.5 us; the launch traced here: 32.2 us
  Pallas kernels  27.2 us (84%)
  local copies, waits for them, and re-layouts  4.33 us (13%)
  between operations  0.65 us (2%)
    pallas_call x1, Pallas kernels, call_of_four(): pl.pallas_call(functools.partial(kernel_of_four, (n_band, n_win, chunk)),...  27.2 us
    unnamed x10, local copies, waits for them, and re-layouts  4.33 us

profile of v2, /device:TPU:11, one launch (start us, length us, event | category | flops | bytes accessed | tf_op | source)
XLA Modules:
  0.0 32.2 jit_solution(7511953032147110634)
XLA Ops:
  0.6 0.0 copy-start.3
  0.6 0.7 %copy-done.3 = f32[256]{0:T(256)S(1)} copy-done((f32[256]{0:T(256)S(1)}, f32[256]{0:T(256)}, u32[]{:S(2)}) %copy-start.3) | copy-done | bytes 1048
  1.3 0.0 copy-start
  1.3 1.0 %copy-done = bf16[2,256,320]{1,2,0:T(8,128)(2,1)S(1)} copy-done((bf16[2,256,320]{1,2,0:T(8,128)(2,1)S(1)}, bf16[2,256,320]{1,2,0:T(8,128)(2,1)}, u32[]{:S(2)}) %copy-start) | copy-done | bytes 327704
  2.3 0.0 copy-start.1
  2.3 0.7 %copy-done.1 = s32[320,8]{0,1:T(8,128)S(1)} copy-done((s32[320,8]{0,1:T(8,128)S(1)}, s32[320,8]{0,1:T(8,128)}, u32[]{:S(2)}) %copy-start.1) | copy-done | bytes 10264
  3.0 0.0 copy-start.2
  3.0 0.7 %copy-done.2 = s32[4,320]{1,0:T(4,128)S(1)} copy-done((s32[4,320]{1,0:T(4,128)S(1)}, s32[4,320]{1,0:T(4,128)}, u32[]{:S(2)}) %copy-start.2) | copy-done | bytes 5144
  3.7 27.2 %coherence_of_four.1 = (f32[80,2,320]{2,1,0:T(2,128)S(1)}, f32[8,80]{1,0:T(8,128)S(1)}) custom-call(bf16[2,320,256]{2,1,0:T(8,128)(2,1)S(1)} %bitcast.4, s32[4,320]{1,0:T(4,128)S(1)} %copy-done.2, f32[1,256]{1,0:T(1,128)S(1)} %bitcast.7, s32[8,320]{1,0:T(8,128)S(1)} %bitcast.5), custom_call_target="tpu_custom_call" | custom-call | tf_op jit(solution)/shard_map/coherence_of_four/pallas_call | solution.py:515
  30.9 0.7 %copy.8 = f32[80,2,320]{2,1,0:T(2,128)} copy(f32[80,2,320]{2,1,0:T(2,128)S(1)} %get-tuple-element.8) | data formatting | bytes 409600
  31.6 0.6 %copy.9 = f32[80,8]{0,1:T(8,128)} copy(f32[80,8]{0,1:T(8,128)S(1)} %bitcast.6) | data formatting | bytes 5120
Async XLA Ops:
  0.6 0.7 %copy-start.3 = (f32[256]{0:T(256)S(1)}, f32[256]{0:T(256)}, u32[]{:S(2)}) copy-start(f32[256]{0:T(256)} %param.6) | copy-start | bytes 3076
  1.3 1.0 %copy-start = (bf16[2,256,320]{1,2,0:T(8,128)(2,1)S(1)}, bf16[2,256,320]{1,2,0:T(8,128)(2,1)}, u32[]{:S(2)}) copy-start(bf16[2,256,320]{1,2,0:T(8,128)(2,1)} %param.4) | copy-start | bytes 983044
  2.3 0.7 %copy-start.1 = (s32[320,8]{0,1:T(8,128)S(1)}, s32[320,8]{0,1:T(8,128)}, u32[]{:S(2)}) copy-start(s32[320,8]{0,1:T(8,128)} %param.7) | copy-start | bytes 30724
  3.0 0.7 %copy-start.2 = (s32[4,320]{1,0:T(4,128)S(1)}, s32[4,320]{1,0:T(4,128)}, u32[]{:S(2)}) copy-start(s32[4,320]{1,0:T(4,128)} %valid_ref.1) | copy-start | bytes 15364

commit v3 on v2

--- a/solution.py
+++ b/solution.py
@@ -14,6 +14,7 @@
 COS = (1.0, -0.49999988079071045, 0.041666485369205475, -0.0013887780951336026,
        2.4769393348833546e-05, -2.707419355374441e-07, 1.7227314019763185e-09)
 FLAG_ROWS = 8
+VMEM_OF_FOUR = 60 * 1024 * 1024
 
 
 def horner(coefficients, u):
@@ -220,19 +221,22 @@
 
 
 NEXT, OPPOSITE = 0, 1
+FIRST, LAST, PAIR, LATE = "first", "last", "pair", "late"
 ARRIVALS = (
-    ((NEXT, 0), (NEXT, 1), (NEXT, 2), (NEXT, 3)),
-    ((NEXT, 0), (NEXT, 1), (OPPOSITE, 2), (NEXT, 2), (OPPOSITE, 3), (NEXT, 3)),
-    ((OPPOSITE, 0), (NEXT, 2), (OPPOSITE, 1), (NEXT, 3),
-     (OPPOSITE, 2), (NEXT, 0), (OPPOSITE, 3), (NEXT, 1)),
-    ((OPPOSITE, 0), (OPPOSITE, 1), (NEXT, 0), (NEXT, 1), (NEXT, 2), (NEXT, 3)),
+    ((NEXT, 0), (NEXT, 1), FIRST, (NEXT, 2), (NEXT, 3), LAST),
+    ((NEXT, 0), LATE, (NEXT, 1), FIRST, (NEXT, 2), (NEXT, 3), LAST,
+     (OPPOSITE, 2), (OPPOSITE, 3), PAIR),
+    ((NEXT, 2), (OPPOSITE, 0), (NEXT, 3), (OPPOSITE, 1), (NEXT, 0), (NEXT, 1), FIRST,
+     (OPPOSITE, 2), (OPPOSITE, 3), LAST, PAIR),
+    ((NEXT, 0), (NEXT, 1), FIRST, (OPPOSITE, 0), (OPPOSITE, 1), PAIR, (NEXT, 2), (NEXT, 3), LAST),
 )
 OWN_SENDS = (
     ((2, OPPOSITE, 0), (2, OPPOSITE, 1), (2, OPPOSITE, 2), (2, OPPOSITE, 3)),
-    ((3, OPPOSITE, 0), (0, NEXT, 0), (3, OPPOSITE, 1), (0, NEXT, 1), (0, NEXT, 2), (0, NEXT, 3)),
+    ((0, NEXT, 0), (0, NEXT, 1), (0, NEXT, 2), (0, NEXT, 3), (3, OPPOSITE, 0), (3, OPPOSITE, 1)),
     ((1, NEXT, 0), (1, NEXT, 1), (1, NEXT, 2), (1, NEXT, 3)),
     ((2, NEXT, 2), (2, NEXT, 3), (2, NEXT, 0), (2, NEXT, 1)),
 )
+AT_ONCE = (2, 4, 4, 2)
 RELAYS = {
     (OPPOSITE, 0): (3, NEXT), (OPPOSITE, 1): (3, NEXT),
     (OPPOSITE, 2): (3, NEXT), (OPPOSITE, 3): (3, NEXT),
@@ -244,7 +248,7 @@
 def kernel_of_four(
     plan, phase_ref, valid_ref, gain_ref, index_ref, coh_ref, cross_ref,
     phase, gain, index, valid, far_phase, flags, turn, columns,
-    own_side, far_own, far_next, own_opposite, far_opposite, inverse,
+    own_side, far_own, far_next, own_opposite, far_opposite, inverse, first_term,
     part, part_in, xpart, xpart_in, xopposite_in,
     load_sem, small_send, small_recv, own_send, relay_send, recv,
     sum_send, sum_recv, xsend, xrecv, ysend, yrecv,
@@ -323,7 +327,7 @@
     for z in range(4):
         @pl.when(at == z)
         def _():
-            for copy in own_copies(z):
+            for copy in own_copies(z)[: AT_ONCE[z]]:
                 copy.start()
 
     def window_row(slot, w):
@@ -361,20 +365,23 @@
 
     sums = []
 
-    def coherence_piece(k, far, scale):
-        ratio = dot_t(own_side[0], far[0]) * window_row(k, 0)
-        for w in range(1, wins):
-            ratio += dot_t(own_side[w], far[w]) * window_row(k, w)
-        ratio = ratio * scale
+    for k in range(2):
+        for d in range(1, owners):
+            sums.append(
+                remote(
+                    part.at[k, owner_of(d)], part_in.at[k, d - 1],
+                    sum_send.at[k, d - 1], sum_recv.at[k, d - 1], owner_device(d),
+                )
+            )
+
+    def window_term(k, far, w):
+        return dot_t(own_side[w], far[w]) * window_row(k, w)
+
+    def send_coherence(k, ratio):
         for r in range(owners):
             part[k, r] = ratio[r * own_rows : (r + 1) * own_rows, :].astype(jnp.bfloat16)
-        for d in range(1, owners):
-            copy = remote(
-                part.at[k, owner_of(d)], part_in.at[k, d - 1],
-                sum_send.at[k, d - 1], sum_recv.at[k, d - 1], owner_device(d),
-            )
+        for copy in sums[k * (owners - 1) : (k + 1) * (owners - 1)]:
             copy.start()
-            sums.append(copy)
 
     def own_xcopies():
         return [
@@ -417,7 +424,14 @@
         loads[3 + w].wait()
         for q in (2 * w, 2 * w + 1):
             trig(phase, far_own, own_side, 0, q)
-    coherence_piece(0, far_own, inverse_counts(0, 0))
+        for z in (0, 3):
+            @pl.when(at == z)
+            def _():
+                copies = own_copies(z)
+                copies[w].wait_send()
+                copies[2 + w].start()
+    own_terms = window_term(0, far_own, 0) + window_term(0, far_own, 1)
+    send_coherence(0, own_terms * inverse_counts(0, 0))
 
     for copy in smalls:
         copy.wait_recv()
@@ -441,28 +455,34 @@
         @pl.when(at == z)
         def _():
             relays = relay_copies() if z == 2 else {}
-            for slot, q in ARRIVALS[z]:
-                landed = quarter(far_phase.at[slot], q)
-                remote(
-                    landed, landed, relay_send.at[0], recv.at[slot, q], {"loop": (z + 1) % 4}
-                ).wait_recv()
-                if (slot, q) in relays:
-                    relays[slot, q].start()
-                if slot == NEXT:
-                    trig(far_phase.at[NEXT], far_next, None, None, q)
+            for step in ARRIVALS[z]:
+                if step == FIRST:
+                    first_term[...] = window_term(1, far_next, 0)
+                elif step == LAST:
+                    terms = first_term[...] + window_term(1, far_next, 1)
+                    send_coherence(1, terms * inverse[0])
+                elif step == PAIR:
+                    crossing_piece(1, far_own, own_opposite, 0, PAIR_WINDOWS[z])
+                    for copy in opposite_xcopies():
+                        copy.start()
+                    crossing_piece(0, far_opposite, own_side, 1, PAIR_WINDOWS[z])
+                    for copy in own_xcopies():
+                        copy.start()
+                elif step == LATE:
+                    for copy in own_copies(z)[AT_ONCE[z] :]:
+                        copy.start()
                 else:
-                    trig(far_phase.at[OPPOSITE], far_opposite, own_opposite, 1, q)
-
-    coherence_piece(1, far_next, inverse[0])
-    for z in range(1, 4):
-        @pl.when(at == z)
-        def _():
-            crossing_piece(1, far_own, own_opposite, 0, PAIR_WINDOWS[z])
-            for copy in opposite_xcopies():
-                copy.start()
-            crossing_piece(0, far_opposite, own_side, 1, PAIR_WINDOWS[z])
-            for copy in own_xcopies():
-                copy.start()
+                    slot, q = step
+                    landed = quarter(far_phase.at[slot], q)
+                    remote(
+                        landed, landed, relay_send.at[0], recv.at[slot, q], {"loop": (z + 1) % 4}
+                    ).wait_recv()
+                    if step in relays:
+                        relays[step].start()
+                    if slot == NEXT:
+                        trig(far_phase.at[NEXT], far_next, None, None, q)
+                    else:
+                        trig(far_phase.at[OPPOSITE], far_opposite, own_opposite, 1, q)
 
     for k in range(2):
         total = part[k, owner_at].astype(jnp.float32)
@@ -485,7 +505,7 @@
                     copy.wait_recv()
                     total += xopposite_in[d]
             cross_ref[...] = total[:, 0:own_rows]
-            for copy in own_copies(z):
+            for copy in own_copies(z)[2 if z in (0, 3) else 0 :]:
                 copy.wait_send()
             if z == 2:
                 for copy in relay_copies().values():
@@ -531,6 +551,7 @@
             pltpu.VMEM((2, channels, 128), jnp.float32),
             sides, sides, sides, sides, sides,
             pltpu.VMEM((3, channels, channels), jnp.float32),
+            pltpu.VMEM((channels, channels), jnp.float32),
             pltpu.VMEM((2, owners, own_rows, channels), jnp.bfloat16),
             pltpu.VMEM((2, owners - 1, own_rows, channels), jnp.bfloat16),
             pltpu.VMEM((2, owners, near, lanes), jnp.float32),
@@ -541,7 +562,7 @@
             dma((owners - 1,)), dma((owners - 1,)), dma((owners,)), dma((owners,)),
         ],
         compiler_params=pltpu.CompilerParams(
-            collective_id=1, has_side_effects=True, vmem_limit_bytes=48 * 1024 * 1024
+            collective_id=1, has_side_effects=True, vmem_limit_bytes=VMEM_OF_FOUR
         ),
         name="coherence_of_four",
     )(phases, valid, gain, index)

time: 32.5 us -> 29.7 us (0.914)
  the two profiles are of different devices: /device:TPU:11 before, /device:TPU:25 now
where the time goes in v3:
time: 29.7 us; the launch traced here: 29.6 us
  Pallas kernels  26.7 us (90%)
  local copies, waits for them, and re-layouts  2.29 us (8%)
  between operations  0.65 us (2%)
    pallas_call x1, Pallas kernels, call_of_four(): pl.pallas_call(functools.partial(kernel_of_four, (n_band, n_win, chunk)),...  26.7 us
    unnamed x4, local copies, waits for them, and re-layouts  2.29 us

profile of v3, /device:TPU:25, one launch (start us, length us, event | category | flops | bytes accessed | tf_op | source)
XLA Modules:
  0.0 29.6 jit_solution(16983998057268639621)
XLA Ops:
  0.6 26.7 %coherence_of_four.1 = (f32[80,2,320]{2,1,0:T(2,128)}, f32[8,80]{1,0:T(8,128)}) custom-call(bf16[2,320,256]{2,1,0:T(8,128)(2,1)} %bitcast.4, s32[4,320]{1,0:T(4,128)} %valid_ref.1, f32[1,256]{1,0:T(1,128)} %bitcast.7, s32[8,320]{1,0:T(8,128)} %bitcast.5), custom_call_target="tpu_custom_call" | custom-call | tf_op jit(solution)/shard_map/coherence_of_four/pallas_call | solution.py:535
  27.3 0.0 copy-start
  27.3 1.7 %copy.8 = f32[80,2,320]{2,1,0:T(2,128)} copy(f32[80,2,320]{2,1,0:T(2,128)} %get-tuple-element.8) | data formatting | bytes 409600
  29.0 0.0 copy-done
  29.0 0.6 %copy.9 = f32[80,8]{0,1:T(8,128)} copy(f32[80,8]{0,1:T(8,128)S(1)} %bitcast.6) | data formatting | bytes 5120
Async XLA Ops:
  27.3 1.7 %copy-start = (f32[8,80]{1,0:T(8,128)S(1)}, f32[8,80]{1,0:T(8,128)}, u32[]{:S(2)}) copy-start(f32[8,80]{1,0:T(8,128)} %get-tuple-element.5) | copy-start | bytes 7684

commit v4 on v3

--- a/solution.py
+++ b/solution.py
@@ -226,22 +226,18 @@
     ((NEXT, 0), (NEXT, 1), FIRST, (NEXT, 2), (NEXT, 3), LAST),
     ((NEXT, 0), LATE, (NEXT, 1), FIRST, (NEXT, 2), (NEXT, 3), LAST,
      (OPPOSITE, 2), (OPPOSITE, 3), PAIR),
-    ((NEXT, 2), (OPPOSITE, 0), (NEXT, 3), (OPPOSITE, 1), (NEXT, 0), (NEXT, 1), FIRST,
-     (OPPOSITE, 2), (OPPOSITE, 3), LAST, PAIR),
+    ((OPPOSITE, 2), (OPPOSITE, 3), (OPPOSITE, 0), (OPPOSITE, 1),
+     (NEXT, 0), (NEXT, 1), FIRST, (NEXT, 2), (NEXT, 3), LAST, PAIR),
     ((NEXT, 0), (NEXT, 1), FIRST, (OPPOSITE, 0), (OPPOSITE, 1), PAIR, (NEXT, 2), (NEXT, 3), LAST),
 )
 OWN_SENDS = (
     ((2, OPPOSITE, 0), (2, OPPOSITE, 1), (2, OPPOSITE, 2), (2, OPPOSITE, 3)),
     ((0, NEXT, 0), (0, NEXT, 1), (0, NEXT, 2), (0, NEXT, 3), (3, OPPOSITE, 0), (3, OPPOSITE, 1)),
     ((1, NEXT, 0), (1, NEXT, 1), (1, NEXT, 2), (1, NEXT, 3)),
-    ((2, NEXT, 2), (2, NEXT, 3), (2, NEXT, 0), (2, NEXT, 1)),
+    ((1, OPPOSITE, 2), (1, OPPOSITE, 3), (2, NEXT, 0), (2, NEXT, 1), (2, NEXT, 2), (2, NEXT, 3)),
 )
-AT_ONCE = (2, 4, 4, 2)
-RELAYS = {
-    (OPPOSITE, 0): (3, NEXT), (OPPOSITE, 1): (3, NEXT),
-    (OPPOSITE, 2): (3, NEXT), (OPPOSITE, 3): (3, NEXT),
-    (NEXT, 2): (1, OPPOSITE), (NEXT, 3): (1, OPPOSITE),
-}
+AT_ONCE = (2, 4, 4, 6)
+PASSED_EARLY = (0, 1)
 PAIR_WINDOWS = ((), (1,), (0, 1), (0,))
 
 
@@ -424,12 +420,30 @@
         loads[3 + w].wait()
         for q in (2 * w, 2 * w + 1):
             trig(phase, far_own, own_side, 0, q)
-        for z in (0, 3):
-            @pl.when(at == z)
-            def _():
-                copies = own_copies(z)
-                copies[w].wait_send()
-                copies[2 + w].start()
+        @pl.when(at == 0)
+        def _():
+            copies = own_copies(0)
+            copies[w].wait_send()
+            copies[2 + w].start()
+
+    def relay_copy(q):
+        return remote(
+            quarter(far_phase.at[OPPOSITE], q), quarter(far_phase.at[NEXT], q),
+            relay_send.at[q], recv.at[NEXT, q], {"loop": 3},
+        )
+
+    def await_quarter(slot, q):
+        landed = quarter(far_phase.at[slot], q)
+        remote(
+            landed, landed, relay_send.at[q], recv.at[slot, q], {"loop": lax.rem(at + 1, 4)}
+        ).wait_recv()
+
+    @pl.when(at == 2)
+    def _():
+        for q in PASSED_EARLY:
+            await_quarter(OPPOSITE, q)
+            relay_copy(q).start()
+
     own_terms = window_term(0, far_own, 0) + window_term(0, far_own, 1)
     send_coherence(0, own_terms * inverse_counts(0, 0))
 
@@ -442,19 +456,9 @@
     inverse[1] = inverse_counts(1, 0)
     inverse[2] = inverse_counts(0, 2)
 
-    def relay_copies():
-        copies = {}
-        for n, ((slot, q), (target, there)) in enumerate(sorted(RELAYS.items())):
-            copies[slot, q] = remote(
-                quarter(far_phase.at[slot], q), quarter(far_phase.at[there], q),
-                relay_send.at[n], recv.at[there, q], {"loop": target},
-            )
-        return copies
-
     for z in range(4):
         @pl.when(at == z)
         def _():
-            relays = relay_copies() if z == 2 else {}
             for step in ARRIVALS[z]:
                 if step == FIRST:
                     first_term[...] = window_term(1, far_next, 0)
@@ -473,12 +477,11 @@
                         copy.start()
                 else:
                     slot, q = step
-                    landed = quarter(far_phase.at[slot], q)
-                    remote(
-                        landed, landed, relay_send.at[0], recv.at[slot, q], {"loop": (z + 1) % 4}
-                    ).wait_recv()
-                    if step in relays:
-                        relays[step].start()
+                    passed = z == 2 and slot == OPPOSITE
+                    if not (passed and q in PASSED_EARLY):
+                        await_quarter(slot, q)
+                        if passed:
+                            relay_copy(q).start()
                     if slot == NEXT:
                         trig(far_phase.at[NEXT], far_next, None, None, q)
                     else:
@@ -505,11 +508,11 @@
                     copy.wait_recv()
                     total += xopposite_in[d]
             cross_ref[...] = total[:, 0:own_rows]
-            for copy in own_copies(z)[2 if z in (0, 3) else 0 :]:
+            for copy in own_copies(z)[2 if z == 0 else 0 :]:
                 copy.wait_send()
             if z == 2:
-                for copy in relay_copies().values():
-                    copy.wait_send()
+                for q in range(4):
+                    relay_copy(q).wait_send()
             if z != 0:
                 for copy in own_xcopies() + opposite_xcopies():
                     copy.wait_send()
@@ -557,7 +560,7 @@
             pltpu.VMEM((2, owners, near, lanes), jnp.float32),
             pltpu.VMEM((owners - 1, near, lanes), jnp.float32),
             pltpu.VMEM((owners, near, lanes), jnp.float32),
-            dma((3 + wins,)), dma((3,)), dma((3,)), dma((6,)), dma((6,)), dma((2, 4)),
+            dma((3 + wins,)), dma((3,)), dma((3,)), dma((6,)), dma((4,)), dma((2, 4)),
             dma((2, owners - 1)), dma((2, owners - 1)),
             dma((owners - 1,)), dma((owners - 1,)), dma((owners,)), dma((owners,)),
         ],

time: 29.7 us -> 29.5 us (level)
  the two profiles are of different devices: /device:TPU:25 before, /device:TPU:29 now
where the time goes in v4:
time: 29.5 us; the launch traced here: 29.4 us
  Pallas kernels  26.4 us (89%)
  local copies, waits for them, and re-layouts  2.29 us (8%)
  between operations  0.65 us (2%)
    pallas_call x1, Pallas kernels, call_of_four(): pl.pallas_call(functools.partial(kernel_of_four, (n_band, n_win, chunk)),...  26.4 us
    unnamed x4, local copies, waits for them, and re-layouts  2.29 us

profile of v4, /device:TPU:29, one launch (start us, length us, event | category | flops | bytes accessed | tf_op | source)
XLA Modules:
  0.0 29.4 jit_solution(7801307141286879203)
XLA Ops:
  0.6 26.4 %coherence_of_four.1 = (f32[80,2,320]{2,1,0:T(2,128)}, f32[8,80]{1,0:T(8,128)}) custom-call(bf16[2,320,256]{2,1,0:T(8,128)(2,1)} %bitcast.4, s32[4,320]{1,0:T(4,128)} %valid_ref.1, f32[1,256]{1,0:T(1,128)} %bitcast.7, s32[8,320]{1,0:T(8,128)} %bitcast.5), custom_call_target="tpu_custom_call" | custom-call | tf_op jit(solution)/shard_map/coherence_of_four/pallas_call | solution.py:538
  27.1 0.0 copy-start
  27.1 1.7 %copy.8 = f32[80,2,320]{2,1,0:T(2,128)} copy(f32[80,2,320]{2,1,0:T(2,128)} %get-tuple-element.8) | data formatting | bytes 409600
  28.8 0.0 copy-done
  28.8 0.6 %copy.9 = f32[80,8]{0,1:T(8,128)} copy(f32[80,8]{0,1:T(8,128)S(1)} %bitcast.6) | data formatting | bytes 5120
Async XLA Ops:
  27.1 1.7 %copy-start = (f32[8,80]{1,0:T(8,128)S(1)}, f32[8,80]{1,0:T(8,128)}, u32[]{:S(2)}) copy-start(f32[8,80]{1,0:T(8,128)} %get-tuple-element.5) | copy-start | bytes 7684
